TPU v7x, 128 devices: a whole 4x4x4 slice. The times are simulated.
128 devices in a mesh: band: 32 (over y_hi, x, z), rep: 4 (over y_lo, core).
Axes of the slice: x: 4, y: 4 (y_hi: 2, y_lo: 2; y = y_hi * 2 + y_lo), z: 4, core: 2. Of those that a mesh axis runs over, the one named last changes fastest.
Arguments:
- feats: bfloat16 [524288, 128], P(('band', 'rep')), may hold values from -6 to 6
- tile_vals: bfloat16 [4096, 3, 128, 128], P(('band', 'rep')), may hold values from -0.3125 to 0.3125
- tile_offs: int32 [4096, 3], P(('band', 'rep')), may hold values from -16 to 16, as said below
- w_in: bfloat16 [2, 256, 128], replicated, may hold values from -0.375 to 0.375
- bias_in: float32 [2, 128], replicated, may hold values from -3 to 3
- w_out: bfloat16 [2, 128, 128], replicated, may hold values from -0.5 to 0.5
- gain: float32 [2, 128], replicated, may hold values from 0.1 to 1.9
- cot: bfloat16 [524288, 128], P(('band', 'rep')), may hold values from -6 to 6
Outputs:
- out_feats: bfloat16 [524288, 128], P(('band', 'rep'))
- grad_feats: float32 [524288, 128], P(('band', 'rep'))
- grad_w_in: float32 [2, 256, 128], replicated
- grad_bias_in: float32 [2, 128], replicated
- grad_w_out: float32 [2, 128, 128], replicated
- grad_gain: float32 [2, 128], replicated
Inputs may be any that keep to these rules, and one draw needn't show every extreme that they name: `tile_offs`: in every block row slot 0 is 0, slot 1 lies in -16 to -1 and slot 2 in 1 to 16; block rows whose index is a multiple of 16 have -16 and 16.
All inputs are finite; a program needn't handle non-finite values.
Results may differ from a plain program's by a relative error of at most 0.0085.
Values may be sent and summed in bfloat16 or wider, within the bound.
A program may use at most 128 MiB of HBM per device.

v0:
```python
import math

import jax
import jax.numpy as jnp
from jax import lax
from jax.sharding import PartitionSpec as P

HALO_BLK = 16


def from_behind(x, axis, by):
    peers = lax.axis_size(axis)
    return lax.ppermute(x, axis, [(i, (i + by) % peers) for i in range(peers)])


def packed_total(arrays, axis):
    ends = [0]
    for a in arrays:
        ends.append(ends[-1] + a.size)
    subtotal = lax.psum(jnp.concatenate([a.ravel() for a in arrays]), axis)
    return tuple((subtotal[b:e].reshape(a.shape) for a, b, e in zip(arrays, ends, ends[1:])))


def layer_forward(feats_now, agg_now, weight_in, bias_now, weight_out, gain_now):
    joined = jnp.concatenate([feats_now, agg_now], axis=1)
    pre_act = jnp.dot(joined, weight_in, preferred_element_type=jnp.float32) + bias_now
    act_now = jax.nn.silu(pre_act).astype(jnp.bfloat16)
    mixed = jnp.dot(act_now, weight_out, preferred_element_type=jnp.float32)
    centred = mixed - jnp.mean(mixed, axis=1, keepdims=True)
    inv_std = lax.rsqrt(jnp.mean(centred * centred, axis=1, keepdims=True) + 1e-05)
    normed = centred * inv_std
    feats_next = (feats_now.astype(jnp.float32) + normed * gain_now).astype(jnp.bfloat16)
    return (feats_next, (joined, pre_act, act_now, normed, inv_std))


def layer_backward(grad_now, saved, weight_in, weight_out, gain_now):
    joined, pre_act, act_now, normed, inv_std = saved
    feat_width = gain_now.shape[0]
    grad_gain = jnp.sum(grad_now * normed, axis=0)
    grad_norm = grad_now * gain_now
    grad_mix = inv_std * (
        grad_norm
        - jnp.mean(grad_norm, axis=1, keepdims=True)
        - normed * jnp.mean(grad_norm * normed, axis=1, keepdims=True)
    )
    grad_mix_b = grad_mix.astype(jnp.bfloat16)
    grad_wout = lax.dot_general(
        act_now, grad_mix_b, (((0,), (0,)), ((), ())), preferred_element_type=jnp.float32
    )
    grad_act = lax.dot_general(
        grad_mix_b, weight_out, (((1,), (1,)), ((), ())), preferred_element_type=jnp.float32
    )
    sigma = jax.nn.sigmoid(pre_act)
    grad_pre = grad_act * sigma * (1.0 + pre_act * (1.0 - sigma))
    grad_bias = jnp.sum(grad_pre, axis=0)
    grad_pre_b = grad_pre.astype(jnp.bfloat16)
    grad_win = lax.dot_general(
        joined, grad_pre_b, (((0,), (0,)), ((), ())), preferred_element_type=jnp.float32
    )
    grad_cat = lax.dot_general(
        grad_pre_b, weight_in, (((1,), (1,)), ((), ())), preferred_element_type=jnp.float32
    )
    grad_next = grad_now + grad_cat[:, :feat_width]
    grad_agg = grad_cat[:, feat_width:].astype(jnp.bfloat16)
    return (grad_next, grad_agg, grad_win, grad_bias, grad_wout, grad_gain)


def per_device(feats, tile_vals, tile_offs, w_in, bias_in, w_out, gain, cot):
    node_rows = feats.shape[0]
    feat_width = feats.shape[1]
    tile_width = tile_vals.shape[2]
    block_count = node_rows // tile_width
    rim_rows = HALO_BLK * tile_width
    columns = jnp.arange(block_count, dtype=jnp.int32)[:, None] + HALO_BLK + tile_offs
    flat_columns = columns.reshape(-1)
    rim_index = jnp.arange(HALO_BLK, dtype=jnp.int32)
    low_tiles, low_offs = from_behind(
        (tile_vals[block_count - HALO_BLK :, 2], tile_offs[block_count - HALO_BLK :, 2]),
        ("band", "rep"),
        1,
    )
    high_tiles, high_offs = from_behind(
        (tile_vals[:HALO_BLK, 1], tile_offs[:HALO_BLK, 1]), ("band", "rep"), -1
    )
    low_targets = rim_index + low_offs
    high_targets = block_count + HALO_BLK + rim_index + high_offs
    layer_count = w_in.shape[0]
    feats_now = feats
    stored = []
    for layer_idx in range(layer_count):
        from_below = from_behind(feats_now[node_rows - rim_rows :], ("band", "rep"), 1)
        from_above = from_behind(feats_now[:rim_rows], ("band", "rep"), -1)
        blocks = jnp.concatenate([from_below, feats_now, from_above], axis=0).reshape(
            block_count + 2 * HALO_BLK, tile_width, feat_width
        )
        pieces = blocks[columns]
        summed = jnp.einsum("bkij,bkjd->bid", tile_vals, pieces, preferred_element_type=jnp.float32)
        agg_now = summed.astype(jnp.bfloat16).reshape(node_rows, feat_width)
        feats_now, saved = layer_forward(
            feats_now,
            agg_now,
            w_in[layer_idx],
            bias_in[layer_idx],
            w_out[layer_idx],
            gain[layer_idx],
        )
        stored.append(saved)
    grad_now = cot.astype(jnp.float32)
    win_list, bias_list, wout_list, gain_list = ([], [], [], [])
    for layer_idx in reversed(range(layer_count)):
        grad_now, grad_agg, grad_win, grad_bias, grad_wout, grad_gain = layer_backward(
            grad_now, stored[layer_idx], w_in[layer_idx], w_out[layer_idx], gain[layer_idx]
        )
        grad_blocks = grad_agg.reshape(block_count, tile_width, feat_width)
        contrib = jnp.einsum(
            "bkij,bid->bkjd", tile_vals, grad_blocks, preferred_element_type=jnp.float32
        )
        extended = jnp.zeros((block_count + 2 * HALO_BLK, tile_width, feat_width), jnp.float32)
        extended = extended.at[flat_columns].add(contrib.reshape(-1, tile_width, feat_width))
        low_rim = from_behind(grad_agg[node_rows - rim_rows :], ("band", "rep"), 1)
        high_rim = from_behind(grad_agg[:rim_rows], ("band", "rep"), -1)
        low_contrib = jnp.einsum(
            "bij,bid->bjd",
            low_tiles,
            low_rim.reshape(HALO_BLK, tile_width, feat_width),
            preferred_element_type=jnp.float32,
        )
        high_contrib = jnp.einsum(
            "bij,bid->bjd",
            high_tiles,
            high_rim.reshape(HALO_BLK, tile_width, feat_width),
            preferred_element_type=jnp.float32,
        )
        extended = extended.at[low_targets].add(low_contrib)
        extended = extended.at[high_targets].add(high_contrib)
        grad_now = grad_now + extended.reshape(-1, feat_width)[rim_rows : rim_rows + node_rows]
        win_list.insert(0, grad_win)
        bias_list.insert(0, grad_bias)
        wout_list.insert(0, grad_wout)
        gain_list.insert(0, grad_gain)
    totals = packed_total(
        (jnp.stack(win_list), jnp.stack(bias_list), jnp.stack(wout_list), jnp.stack(gain_list)),
        ("band", "rep"),
    )
    scale_factor = 1.0 / math.sqrt(node_rows * lax.axis_size("band") * lax.axis_size("rep"))
    return (
        feats_now,
        grad_now,
        totals[0] * scale_factor,
        totals[1] * scale_factor,
        totals[2] * scale_factor,
        totals[3] * scale_factor,
    )


def solution(mesh):
    placed = (
        P(("band", "rep"), None),
        P(("band", "rep"), None, None, None),
        P(("band", "rep"), None),
        P(),
        P(),
        P(),
        P(),
        P(("band", "rep"), None),
    )
    return jax.shard_map(
        per_device,
        mesh=mesh,
        in_specs=placed,
        out_specs=(P(("band", "rep"), None), P(("band", "rep"), None), P(), P(), P(), P()),
        check_vma=False,
    )
```

profile of v0, /device:TPU:1, one launch (start us, length us, event | category | flops | bytes accessed | tf_op | source)
XLA Modules:
  0.0 355.5 jit_solution(14039582905119262388)
XLA Ops:
  7.2 1.3 fusion.50
  8.6 2.8 collective-permute-start
  11.3 2.4 slice_bitcast_fusion
  13.7 1.7 collective-permute-start.6
  15.7 5.2 %collective-permute-start.9 = (bf16[16,128,128]{2,1,0:T(8,128)(2,1)}, bf16[16,128,128]{2,1,0:T(8,128)(2,1)}, u32[]{:S(2)}, u32[]{:S(2)}) collective-permute-start(bf16[16,128,128]{2,1,0:T(8,128)(2,1)} %get-tuple-element.27), channel_id=1, source_target_pairs={{0,127},{1,0},{2,1},{3,2},{4,3},{5,4},{6,5},{7,6},{8,7},{9,8},{10,... | collective-permute-start | bytes 1572872 | tf_op jit(solution)/shard_map/ppermute | solution.py:13
  20.9 1.3 copy.40
  23.1 2.4 collective-permute-done.1
  25.5 1.5 pad_maximum_fusion
  27.0 4.4 %gather_fusion = bf16[96,128,128]{2,1,0:T(8,128)(2,1)} fusion(bf16[64,128,128]{2,1,0:T(8,128)(2,1)} %bitcast.158, s32[1024]{0:T(1024)S(1)} %pad_clamp_fusion), kind=kCustom, calls=%fused_computation | custom fusion | bytes 6291840 | tf_op jit(solution)/shard_map/gather | solution.py:96
  31.4 3.0 bitcast_convert_fusion.1
  34.4 2.0 multiply_convert_fusion.2
  38.9 1.1 fusion.49
  40.3 4.3 %collective-permute-start.3 = (bf16[2048,128]{0,1:T(8,128)(2,1)}, bf16[2048,128]{0,1:T(8,128)(2,1)}, u32[]{:S(2)}, u32[]{:S(2)}) collective-permute-start(bf16[2048,128]{0,1:T(8,128)(2,1)} %get-tuple-element.36), channel_id=1, source_target_pairs={{0,127},{1,0},{2,1},{3,2},{4,3},{5,4},{6,5},{7,6},{8,7},{9,8},{10,... | collective-permute-start | bytes 1572872 | tf_op jit(solution)/shard_map/ppermute | solution.py:13
  44.6 2.3 copy.44
  46.9 7.2 %collective-permute-start.7 = (s32[16]{0:T(128)S(1)}, s32[16]{0:T(128)S(1)}, u32[]{:S(2)}, u32[]{:S(2)}) collective-permute-start(s32[16]{0:T(128)S(1)} %get-tuple-element.41), channel_id=1, source_target_pairs={{0,127},{1,0},{2,1},{3,2},{4,3},{5,4},{6,5},{7,6},{8,7},{9,8},{10,... | collective-permute-start | bytes 200 | tf_op jit(solution)/shard_map/ppermute | solution.py:13
  54.1 1.5 collective-permute-done.7
  55.6 3.0 pad_maximum_fusion.2
  58.6 4.1 %copy.74 = bf16[8192,128]{1,0:T(8,128)(2,1)} copy(bf16[8192,128]{0,1:T(8,128)(2,1)} %pad_maximum_fusion.2) | data formatting | bytes 4194304 | tf_op jit(solution)/shard_map/reshape | solution.py:93
  62.7 4.3 %gather_fusion.1 = bf16[96,128,128]{2,1,0:T(8,128)(2,1)} fusion(bf16[64,128,128]{2,1,0:T(8,128)(2,1)} %bitcast.159, s32[1024]{0:T(1024)S(1)} %pad_clamp_fusion), kind=kCustom, calls=%fused_computation.1 | custom fusion | bytes 6291840 | tf_op jit(solution)/shard_map/gather | solution.py:96
  67.0 3.8 %bitcast_convert_fusion = bf16[32,128,128]{1,2,0:T(8,128)(2,1)} fusion(bf16[32,3,128,128]{3,2,1,0:T(8,128)(2,1)S(1)} %copy-done, bf16[32,3,128,128]{3,2,1,0:T(8,128)(2,1)} %bitcast.160), kind=kOutput, calls=%fused_computation.30 | convolution fusion | flops 403177472 | bytes 7340032 | tf_op jit(solution)/shard_map/bkij,bkjd->bid/dot_general | solution.py:97
  70.8 2.3 copy.75
  73.1 2.5 multiply_convert_fusion.1
  78.2 1.9 fusion.7
  81.1 2.6 fusion.53
  84.9 3.7 %fusion.57 = f32[32,128,3,128]{3,1,2,0:T(8,128)} fusion(bf16[32,128,128,1]{2,1,3,0:T(8,128)(2,1)S(1)} %bitcast.164, bf16[32,3,128,128]{3,2,1,0:T(8,128)(2,1)S(1)} %copy-done), kind=kOutput, calls=%fused_computation.130 | convolution fusion | flops 402653184 | bytes 10485760 | tf_op jit(solution)/shard_map/bkij,bid->bkjd/dot_general | solution.py:115
  88.6 6.6 %copy.48 = f32[96,128,128]{2,1,0:T(8,128)} copy(f32[96,128,128]{1,2,0:T(8,128)} %bitcast.157) | data formatting | bytes 12582912 | tf_op jit(solution)/shard_map/reshape | solution.py:119
  95.1 3.3 collective-permute-start.8
  98.4 3.1 slice.162
  101.5 3.0 copy.82
  104.5 2.3 copy.64
  106.7 2.5 broadcast.125.clone
  109.3 19.9 %scatter_fusion = f32[64,128,128]{2,1,0:T(8,128)} fusion(f32[64,128,128]{2,1,0:T(8,128)} %broadcast.125.clone, s32[96]{0:T(128)S(1)} %fusion.41, f32[96,128,128]{2,1,0:T(8,128)} %copy.48), kind=kCustom, calls=%fused_computation.2 | custom fusion | flops 1572864 | bytes 18874752 | tf_op jit(solution)/shard_map/scatter-add | solution.py:119
  129.2 2.2 convolution_bitcast_fusion.4
  131.4 2.0 fusion.14
  133.4 2.6 convolution_bitcast_fusion.3
  136.0 2.6 copy.51
  138.5 2.5 convolution_bitcast_fusion.2
  141.1 2.6 copy.54
  143.7 3.8 %scatter_fusion.1 = f32[64,128,128]{2,1,0:T(8,128)} fusion(f32[64,128,128]{2,1,0:T(8,128)} %scatter_fusion, s32[16]{0:T(128)S(1)} %compare_select_fusion.2, f32[16,128,128]{2,1,0:T(8,128)} %copy.51), kind=kCustom, calls=%fused_computation.3 | custom fusion | flops 262144 | bytes 3145792 | tf_op jit(solution)/shard_map/scatter-add | solution.py:134
  147.4 3.8 %scatter_fusion.2 = f32[64,128,128]{2,1,0:T(8,128)} fusion(f32[64,128,128]{2,1,0:T(8,128)} %scatter_fusion.1, s32[16]{0:T(128)S(1)} %compare_select_fusion.1, f32[16,128,128]{2,1,0:T(8,128)} %copy.54), kind=kCustom, calls=%fused_computation.4 | custom fusion | flops 262144 | bytes 3145792 | tf_op jit(solution)/shard_map/scatter-add | solution.py:135
  151.2 3.1 slice.166
  154.4 2.9 copy.78
  157.3 4.2 %multiply_reduce_fusion = (f32[128]{0:T(128)S(1)}, f32[4096]{0:T(1024)S(1)}, f32[4096]{0:T(1024)S(1)}, f32[4096,128]{0,1:T(8,128)S(1)}) fusion(f32[4096,128]{0,1:T(8,128)} %copy-done.1, f32[4096]{0:T(1024)S(1)} %add_rsqrt_fusion.1, f32[4096]{0:T(1024)S(1)} %broadcast_multiply_fusion.5, f32[128]{0:T(128)S(1)} %get-tuple-element.44, f32[4096,128]{0,1:T(8,128)} %copy.78, ...), kind=kLoop, calls=%fused_computation.32 | loop fusion | flops 5758848 | bytes 9503744 | tf_op jit(solution)/shard_map/reduce_sum | solution.py:39
  167.5 3.4 fusion.54
  171.8 1.3 slice.168
  173.1 3.7 %fusion.58 = f32[32,128,3,128]{3,1,2,0:T(8,128)} fusion(bf16[32,128,128,1]{2,1,3,0:T(8,128)(2,1)S(1)} %bitcast.166, bf16[32,3,128,128]{3,2,1,0:T(8,128)(2,1)S(1)} %copy-done), kind=kOutput, calls=%fused_computation.131 | convolution fusion | flops 402653184 | bytes 10485760 | tf_op jit(solution)/shard_map/bkij,bid->bkjd/dot_general | solution.py:115
  177.6 6.6 %copy.58 = f32[96,128,128]{2,1,0:T(8,128)} copy(f32[96,128,128]{1,2,0:T(8,128)} %bitcast.156) | data formatting | bytes 12582912 | tf_op jit(solution)/shard_map/reshape | solution.py:119
  184.2 7.3 %collective-permute-start.11 = (bf16[2048,128]{1,0:T(8,128)(2,1)S(1)}, bf16[2048,128]{1,0:T(8,128)(2,1)S(1)}, u32[]{:S(2)}, u32[]{:S(2)}) collective-permute-start(bf16[2048,128]{1,0:T(8,128)(2,1)S(1)} %get-tuple-element.31), channel_id=1, source_target_pairs={{0,127},{1,0},{2,1},{3,2},{4,3},{5,4},{6,5},{7,6},{8,7},{9,8},{10,... | collective-permute-start | bytes 1572872 | tf_op jit(solution)/shard_map/ppermute | solution.py:13
  191.5 1.7 slice.167
  193.2 1.9 copy.85
  195.1 2.5 broadcast.125
  197.7 20.0 %scatter_fusion.3 = f32[64,128,128]{2,1,0:T(8,128)} fusion(f32[64,128,128]{2,1,0:T(8,128)} %broadcast.125, s32[96]{0:T(128)S(1)} %fusion.41, f32[96,128,128]{2,1,0:T(8,128)} %copy.58), kind=kCustom, calls=%fused_computation.5 | custom fusion | flops 1572864 | bytes 18874752 | tf_op jit(solution)/shard_map/scatter-add | solution.py:119
  217.7 102.1 %all-reduce.2.cloned.1.call-done = f32[98816]{0:T(1024)} async-done(((f32[98816]{0:T(1024)}), f32[98816]{0:T(1024)}) %all-reduce.2.cloned.1.call-update) | async-done | bytes 395280 | tf_op jit(solution)/shard_map/psum | solution.py:20
  319.8 1.7 slice_multiply_fusion
  321.5 1.6 slice_multiply_fusion.1
  323.1 1.3 fusion.39
  324.3 1.5 convolution_bitcast_fusion.1
  327.0 1.5 convolution_bitcast_fusion
  328.9 3.3 scatter_fusion.4
  332.3 3.4 scatter_fusion.5
  335.6 3.1 slice.171
  338.8 3.1 copy.81
  341.9 3.9 %add_add_fusion = f32[4096,128]{0,1:T(8,128)} fusion(f32[4096,128]{0,1:T(8,128)} %copy.81, f32[4096,128]{0,1:T(8,128)S(1)} %copy-done.4, f32[4096,128]{0,1:T(8,128)} %copy.85), kind=kLoop, calls=%fused_computation.33 | loop fusion | flops 1048576 | bytes 8388608 | tf_op jit(solution)/shard_map/add | solution.py:136
  345.8 2.9 copy.65
  (118 shorter events, 17.6 us)
Async XLA Ops:
  7.2 13.8 %copy-start.9 = (bf16[4096,128]{1,0:T(8,128)(2,1)S(1)}, bf16[4096,128]{1,0:T(8,128)(2,1)}, u32[]{:S(2)}) copy-start(bf16[4096,128]{1,0:T(8,128)(2,1)} %param.8) | copy-start | bytes 3145732
  7.2 8.3 %copy-start.26 = (s32[32,3]{0,1:T(4,128)S(1)}, s32[32,3]{0,1:T(4,128)}, u32[]{:S(2)}) copy-start(s32[32,3]{0,1:T(4,128)} %param.10) | copy-start | bytes 1156
  7.2 312.6 %all-reduce.2.cloned.1.call-start = ((), (), s32[]{:S(2)}) async-start(), calls=%async_computation | async-start | bytes 794624 | tf_op jit(solution)/shard_map/psum | solution.py:20
  8.6 14.5 %collective-permute-start = (bf16[2048,128]{1,0:T(8,128)(2,1)S(1)}, bf16[2048,128]{1,0:T(8,128)(2,1)S(1)}, u32[]{:S(2)}, u32[]{:S(2)}) collective-permute-start(bf16[2048,128]{1,0:T(8,128)(2,1)S(1)} %get-tuple-element.37), channel_id=1, source_target_pairs={{0,1},{1,2},{2,3},{3,4},{4,5},{5,6},{6,7},{7,8},{8,9},{9,10},{10,1... | collective-permute-start | bytes 1572872 | tf_op jit(solution)/shard_map/ppermute | solution.py:13
  11.3 11.3 %copy-start.27 = (f32[2,128]{1,0:T(2,128)S(1)}, f32[2,128]{1,0:T(2,128)}, u32[]{:S(2)}) copy-start(f32[2,128]{1,0:T(2,128)} %param.12) | copy-start | bytes 3076
  11.3 11.3 %copy-start.28 = (f32[2,128]{1,0:T(2,128)S(1)}, f32[2,128]{1,0:T(2,128)}, u32[]{:S(2)}) copy-start(f32[2,128]{1,0:T(2,128)} %param.14) | copy-start | bytes 3076
  11.3 14.2 %collective-permute-start.1 = (bf16[2048,128]{1,0:T(8,128)(2,1)S(1)}, bf16[2048,128]{1,0:T(8,128)(2,1)S(1)}, u32[]{:S(2)}, u32[]{:S(2)}) collective-permute-start(bf16[2048,128]{1,0:T(8,128)(2,1)S(1)} %get-tuple-element.38), channel_id=1, source_target_pairs={{0,127},{1,0},{2,1},{3,2},{4,3},{5,4},{6,5},{7,6},{8,7},{9,8},{10,... | collective-permute-start | bytes 1572872 | tf_op jit(solution)/shard_map/ppermute | solution.py:13
  13.7 119.6 %collective-permute-start.6 = (bf16[16,128,128]{2,1,0:T(8,128)(2,1)}, bf16[16,128,128]{2,1,0:T(8,128)(2,1)}, u32[]{:S(2)}, u32[]{:S(2)}) collective-permute-start(bf16[16,128,128]{2,1,0:T(8,128)(2,1)} %get-tuple-element.28), channel_id=1, source_target_pairs={{0,1},{1,2},{2,3},{3,4},{4,5},{5,6},{6,7},{7,8},{8,9},{9,10},{10,1... | collective-permute-start | bytes 1572872 | tf_op jit(solution)/shard_map/ppermute | solution.py:13
  15.5 31.4 %collective-permute-start.4 = (s32[16]{0:T(128)S(1)}, s32[16]{0:T(128)S(1)}, u32[]{:S(2)}, u32[]{:S(2)}) collective-permute-start(s32[16]{0:T(128)S(1)} %get-tuple-element.42), channel_id=1, source_target_pairs={{0,1},{1,2},{2,3},{3,4},{4,5},{5,6},{6,7},{7,8},{8,9},{9,10},{10,1... | collective-permute-start | bytes 200 | tf_op jit(solution)/shard_map/ppermute | solution.py:13
  15.7 122.8 %collective-permute-start.9 = (bf16[16,128,128]{2,1,0:T(8,128)(2,1)}, bf16[16,128,128]{2,1,0:T(8,128)(2,1)}, u32[]{:S(2)}, u32[]{:S(2)}) collective-permute-start(bf16[16,128,128]{2,1,0:T(8,128)(2,1)} %get-tuple-element.27), channel_id=1, source_target_pairs={{0,127},{1,0},{2,1},{3,2},{4,3},{5,4},{6,5},{7,6},{8,7},{9,8},{10,... | collective-permute-start | bytes 1572872 | tf_op jit(solution)/shard_map/ppermute | solution.py:13
  27.0 4.4 %copy-start = (bf16[32,3,128,128]{3,2,1,0:T(8,128)(2,1)S(1)}, bf16[32,3,128,128]{3,2,1,0:T(8,128)(2,1)}, u32[]{:S(2)}) copy-start(bf16[32,3,128,128]{3,2,1,0:T(8,128)(2,1)} %param.9) | copy-start | bytes 9437188
  31.4 3.0 copy-start.10
  31.4 3.0 copy-start.23
  34.4 2.1 copy-start.18
  34.4 2.1 copy-start.24
  36.4 1.0 copy-start.13
  36.4 2.0 copy-start.16
  36.9 1.9 copy-start.1
  38.9 1.3 copy-start.6
  40.2 15.4 %collective-permute-start.2 = (bf16[2048,128]{0,1:T(8,128)(2,1)}, bf16[2048,128]{0,1:T(8,128)(2,1)}, u32[]{:S(2)}, u32[]{:S(2)}) collective-permute-start(bf16[2048,128]{0,1:T(8,128)(2,1)} %get-tuple-element.35), channel_id=1, source_target_pairs={{0,1},{1,2},{2,3},{3,4},{4,5},{5,6},{6,7},{7,8},{8,9},{9,10},{10,1... | collective-permute-start | bytes 1572872 | tf_op jit(solution)/shard_map/ppermute | solution.py:13
  40.3 15.3 %collective-permute-start.3 = (bf16[2048,128]{0,1:T(8,128)(2,1)}, bf16[2048,128]{0,1:T(8,128)(2,1)}, u32[]{:S(2)}, u32[]{:S(2)}) collective-permute-start(bf16[2048,128]{0,1:T(8,128)(2,1)} %get-tuple-element.36), channel_id=1, source_target_pairs={{0,127},{1,0},{2,1},{3,2},{4,3},{5,4},{6,5},{7,6},{8,7},{9,8},{10,... | collective-permute-start | bytes 1572872 | tf_op jit(solution)/shard_map/ppermute | solution.py:13
  46.9 8.7 %collective-permute-start.7 = (s32[16]{0:T(128)S(1)}, s32[16]{0:T(128)S(1)}, u32[]{:S(2)}, u32[]{:S(2)}) collective-permute-start(s32[16]{0:T(128)S(1)} %get-tuple-element.41), channel_id=1, source_target_pairs={{0,127},{1,0},{2,1},{3,2},{4,3},{5,4},{6,5},{7,6},{8,7},{9,8},{10,... | collective-permute-start | bytes 200 | tf_op jit(solution)/shard_map/ppermute | solution.py:13
  75.6 1.0 copy-start.15
  75.7 1.6 copy-start.5
  76.7 1.5 copy-start.7
  80.0 1.0 copy-start.17
  81.1 2.7 copy-start.20
  84.9 48.5 %collective-permute-start.5 = (bf16[2048,128]{1,0:T(8,128)(2,1)}, bf16[2048,128]{1,0:T(8,128)(2,1)}, u32[]{:S(2)}, u32[]{:S(2)}) collective-permute-start(bf16[2048,128]{1,0:T(8,128)(2,1)} %get-tuple-element.34), channel_id=1, source_target_pairs={{0,1},{1,2},{2,3},{3,4},{4,5},{5,6},{6,7},{7,8},{8,9},{9,10},{10,1... | collective-permute-start | bytes 1572872 | tf_op jit(solution)/shard_map/ppermute | solution.py:13
  95.1 43.4 %collective-permute-start.8 = (bf16[2048,128]{1,0:T(8,128)(2,1)}, bf16[2048,128]{1,0:T(8,128)(2,1)}, u32[]{:S(2)}, u32[]{:S(2)}) collective-permute-start(bf16[2048,128]{1,0:T(8,128)(2,1)} %get-tuple-element.33), channel_id=1, source_target_pairs={{0,127},{1,0},{2,1},{3,2},{4,3},{5,4},{6,5},{7,6},{8,7},{9,8},{10,... | collective-permute-start | bytes 1572872 | tf_op jit(solution)/shard_map/ppermute | solution.py:13
  129.2 2.2 copy-start.8
  129.2 2.2 copy-start.21
  157.3 4.3 %copy-start.2 = (f32[4096,128]{0,1:T(8,128)S(1)}, f32[4096,128]{0,1:T(8,128)}, u32[]{:S(2)}) copy-start(f32[4096,128]{0,1:T(8,128)} %copy-done.1) | copy-start | bytes 6291460
  161.6 1.3 copy-start.3
  161.6 2.0 copy-start.14
  163.6 0.8 copy-start.25
  163.6 1.6 copy-start.29
  165.2 1.2 copy-start.11
  165.2 1.5 copy-start.19
  173.1 3.7 %copy-start.12 = (bf16[4096,256]{1,0:T(8,128)(2,1)S(1)}, bf16[4096,256]{1,0:T(8,128)(2,1)}, u32[]{:S(2)}) copy-start(bf16[4096,256]{1,0:T(8,128)(2,1)} %get-tuple-element.57) | copy-start | bytes 6291460
  184.2 140.1 %collective-permute-start.10 = (bf16[2048,128]{1,0:T(8,128)(2,1)}, bf16[2048,128]{1,0:T(8,128)(2,1)}, u32[]{:S(2)}, u32[]{:S(2)}) collective-permute-start(bf16[2048,128]{1,0:T(8,128)(2,1)} %get-tuple-element.32), channel_id=1, source_target_pairs={{0,1},{1,2},{2,3},{3,4},{4,5},{5,6},{6,7},{7,8},{8,9},{9,10},{10,1... | collective-permute-start | bytes 1572872 | tf_op jit(solution)/shard_map/ppermute | solution.py:13
  184.2 142.0 %collective-permute-start.11 = (bf16[2048,128]{1,0:T(8,128)(2,1)S(1)}, bf16[2048,128]{1,0:T(8,128)(2,1)S(1)}, u32[]{:S(2)}, u32[]{:S(2)}) collective-permute-start(bf16[2048,128]{1,0:T(8,128)(2,1)S(1)} %get-tuple-element.31), channel_id=1, source_target_pairs={{0,127},{1,0},{2,1},{3,2},{4,3},{5,4},{6,5},{7,6},{8,7},{9,8},{10,... | collective-permute-start | bytes 1572872 | tf_op jit(solution)/shard_map/ppermute | solution.py:13
  326.2 0.8 copy-start.22
  338.8 3.1 copy-start.4
Sparse Core Ops, SparseCore 0:
  171.9 147.8 all-reduce.1
where the time goes:
time: 357 us; the launch traced here: 355 us
  waiting for transfers between devices  106 us (30%)
  local copies, waits for them, and re-layouts  84.6 us (24%)
  other arithmetic  76.5 us (21%)
  matrix products  41.4 us (12%)
  starting transfers between devices  32 us (9%)
  between operations  14.5 us (4%)
    psum x1, waiting for transfers between devices, packed_total(): subtotal = lax.psum(jnp.concatenate([a.ravel() for a in arrays]), axis)  102 us
    scatter-add x2, other arithmetic, per_device(): extended.at[flat_columns].add(contrib.reshape(-1, tile_width, feat_width))  40 us
    ppermute x12, starting transfers between devices, from_behind(): return lax.ppermute(x, axis, [(i, (i + by) % peers) for i in range(peers)])  32 us
    unnamed x66, local copies, waits for them, and re-layouts  19.8 us
    reshape x2, local copies, waits for them, and re-layouts, per_device(): contrib.reshape(-1, tile_width, feat_width)  13.2 us
    slice x4, local copies, waits for them, and re-layouts, per_device(): extended.reshape(-1, feat_width)[rim_rows:rim_rows + node_rows]  12.3 us
    gather x2, local copies, waits for them, and re-layouts, per_device(): pieces = blocks[columns]  8.69 us
    dot_general x2, matrix products, per_device(): jnp.einsum('bkij,bid->bkjd', tile_vals, grad_blocks, preferred_element_ty...  7.38 us
  transfers between devices with their start and end apart: 13, of which 4 were waited for; matrix products, arithmetic and copies ran while one was open for 40% of the time, Pallas kernels for 0%

commit v1 on v0

v1 whole, which is shorter than its diff:
```python
import functools
import math

import jax
import jax.numpy as jnp
from jax import lax
from jax.experimental import pallas as pl
from jax.experimental.pallas import tpu as pltpu
from jax.sharding import PartitionSpec as P

MESH = pl.DeviceIdType.MESH
HALO = 16
ROWS = 32
BLK = 128
CH = 4
NCH = HALO // CH
RB = 2
XZ = 16
LINE = 8
PIECE = 64
WROWS = 48
F32 = jnp.float32
BF16 = jnp.bfloat16

COL1, COL2 = 0, 32
PREV_A, PREV_B, PREV_C = 64, 80, 96
LAST_A, LAST_B, LAST_C = 128, 160, 192
TABLE = 224


def links_kernel(offs, tab):
    def clear(k, carry):
        tab[LAST_A + k] = -1
        return carry

    lax.fori_loop(0, 96, clear, 0)

    def low(i, carry):
        col = HALO + i + offs[i, 1]
        tab[COL1 + i] = col
        tab[PREV_A + i] = tab[LAST_A + col]
        tab[LAST_A + col] = i
        col = i + offs[i, 2]
        tab[COL2 + i] = HALO + col
        tab[PREV_C + i] = tab[LAST_C + col]
        tab[LAST_C + col] = i
        return carry

    lax.fori_loop(0, HALO, low, 0)

    def high(t, carry):
        i = ROWS - 1 - t
        col = i - HALO + offs[i, 2]
        tab[COL2 + i] = 2 * HALO + col
        tab[PREV_B + t] = tab[LAST_B + col]
        tab[LAST_B + col] = t
        col = i + offs[i, 1]
        tab[COL1 + i] = HALO + col
        tab[PREV_C + HALO + t] = tab[LAST_C + col]
        tab[LAST_C + col] = HALO + t
        return carry

    lax.fori_loop(0, HALO, high, 0)


def dot(a, b):
    return jnp.dot(a, b, preferred_element_type=F32)


def dot_nt(a, b):
    return lax.dot_general(a, b, (((1,), (1,)), ((), ())), preferred_element_type=F32)


def dot_tn(a, b):
    return lax.dot_general(a, b, (((0,), (0,)), ((), ())), preferred_element_type=F32)


def main_kernel(
    scale,
    feats, tiles_in, cot_in, tab, w_in, bias, w_out, gain,
    out_feats, grad_feats, out_win, out_bias, out_wout, out_gain,
    tiles, h0, h1, h2, cot, agg0, pre0, act0, xh0, inv0, gacc, gagg,
    seg_a, seg_b, seg_c, out_lo, out_hi, rx_lo, rx_hi, acc_w, acc_s,
    s1, r1, s2, r2, s3, r3,
    local_sem, store_sem, tx_lo_sem, tx_hi_sem, rx_lo_sem, rx_hi_sem,
    s1_sem, r1_sem, s2_sem, r2_sem, s3_sem, r3_sem,
):
    band, rep = lax.axis_index("band"), lax.axis_index("rep")
    n_rep, n_band = 4, 32
    me = band * n_rep + rep
    total = n_rep * n_band

    def place(index):
        return (lax.div(index, n_rep), lax.rem(index, n_rep))

    left = place(lax.rem(me + total - 1, total))
    right = place(lax.rem(me + 1, total))
    y_hi, plane = lax.div(band, XZ), lax.rem(band, XZ)
    line = y_hi * n_rep + rep

    def on_line(index):
        return (lax.div(index, n_rep) * XZ + plane, lax.rem(index, n_rep))

    def on_plane(index):
        return (y_hi * XZ + index, rep)

    barrier = pltpu.get_barrier_semaphore()
    for peer in (left, right):
        pl.semaphore_signal(barrier, inc=1, device_id=peer, device_id_type=MESH)
    for d in range(1, LINE):
        pl.semaphore_signal(barrier, inc=1, device_id=on_line(lax.rem(line + d, LINE)), device_id_type=MESH)
    for d in range(1, XZ):
        pl.semaphore_signal(barrier, inc=1, device_id=on_plane(lax.rem(plane + d, XZ)), device_id_type=MESH)

    get_feats = pltpu.make_async_copy(feats, h0.at[pl.ds(HALO, ROWS)], local_sem.at[0])
    get_tiles = pltpu.make_async_copy(tiles_in, tiles, local_sem.at[1])
    get_cot = pltpu.make_async_copy(cot_in, cot, local_sem.at[2])
    get_feats.start()
    get_tiles.start()
    get_cot.start()
    acc_w[...] = jnp.zeros_like(acc_w)
    acc_s[...] = jnp.zeros_like(acc_s)

    pl.semaphore_wait(barrier, 2 + LINE - 1 + XZ - 1)

    def to_left(x, c, src):
        return pltpu.make_async_remote_copy(
            src_ref=src, dst_ref=rx_hi.at[x, pl.ds(c * CH, CH)], send_sem=tx_lo_sem.at[x, c],
            recv_sem=rx_hi_sem.at[x, c], device_id=left, device_id_type=MESH,
        )

    def to_right(x, c, src):
        return pltpu.make_async_remote_copy(
            src_ref=src, dst_ref=rx_lo.at[x, pl.ds(c * CH, CH)], send_sem=tx_hi_sem.at[x, c],
            recv_sem=rx_lo_sem.at[x, c], device_id=right, device_id_type=MESH,
        )

    sent = []

    def go(copy):
        copy.start()
        sent.append(copy)
        return copy

    def wait_low(x, c):
        to_right(x, c, rx_lo.at[x, pl.ds(c * CH, CH)]).wait_recv()

    def wait_high(x, c):
        to_left(x, c, rx_hi.at[x, pl.ds(c * CH, CH)]).wait_recv()

    for s in range(NCH):
        c = NCH - 1 - s
        go(to_left(0, s, feats.at[pl.ds(s * CH, CH)]))
        go(to_right(0, c, feats.at[pl.ds(HALO + c * CH, CH)]))
    get_feats.wait()
    get_tiles.wait()

    def forward(layer, b, ext):
        own = ext[pl.ds(HALO + b, RB)]
        sums = []
        for r in range(RB):
            tile = tiles[b + r]
            lhs = jnp.concatenate([tile[0], tile[1]], axis=1)
            rhs = jnp.concatenate([own[r], ext[tab[COL1 + b + r]]], axis=0)
            sums.append((dot(lhs, rhs) + dot(tile[2], ext[tab[COL2 + b + r]])).astype(BF16))
        own = own.reshape(RB * BLK, BLK)
        agg = jnp.concatenate(sums, axis=0)
        cat = jnp.concatenate([own, agg], axis=1)
        pre = dot(cat, w_in[layer]) + bias[pl.ds(layer, 1), :]
        sig = 0.5 * jnp.tanh(0.5 * pre) + 0.5
        act = (pre * sig).astype(BF16)
        mix = dot(act, w_out[layer])
        cen = mix - jnp.mean(mix, axis=1, keepdims=True)
        inv = lax.rsqrt(jnp.mean(cen * cen, axis=1, keepdims=True) + 1e-05)
        xhat = cen * inv
        nxt = (own.astype(F32) + xhat * gain[pl.ds(layer, 1), :]).astype(BF16)
        return cat, agg, pre, sig, act, xhat, inv, nxt

    def backward(layer, b, g, cat, pre, sig, act, xhat, inv):
        gg = jnp.sum(g * xhat, axis=0, keepdims=True)
        gx = g * gain[pl.ds(layer, 1), :]
        gmix = inv * (
            gx - jnp.mean(gx, axis=1, keepdims=True) - xhat * jnp.mean(gx * xhat, axis=1, keepdims=True)
        )
        gmix_b = gmix.astype(BF16)
        gact = dot_nt(gmix_b, w_out[layer])
        gpre = gact * sig * (1.0 + pre * (1.0 - sig))
        gb = jnp.sum(gpre, axis=0, keepdims=True)
        gpre_b = gpre.astype(BF16)
        acc_w[layer, pl.ds(0, 256), :] += dot_tn(cat, gpre_b)
        acc_w[layer, pl.ds(256, 128), :] += dot_tn(act, gmix_b)
        acc_s[layer, pl.ds(0, 1), :] += gb
        acc_s[layer, pl.ds(1, 1), :] += gg
        gcat = dot_nt(gpre_b, w_in[layer])
        gacc[pl.ds(b, RB)] = (g + gcat[:, :BLK]).reshape(RB, BLK, BLK)
        gagg[pl.ds(b, RB)] = gcat[:, BLK:].astype(BF16).reshape(RB, BLK, BLK)

    def outward(s, k):
        per = CH // RB
        low = (NCH - 1 - s) * CH + k * RB
        high = HALO + s * CH + (k - per) * RB
        return jnp.where(k < per, low, high)

    def inward(s, k):
        per = CH // RB
        low = s * CH + k * RB
        high = (2 * NCH - 1 - s) * CH + (k - per) * RB
        return jnp.where(k < per, low, high)

    for s in range(NCH):
        c = NCH - 1 - s
        wait_low(0, c)
        wait_high(0, s)
        h0[pl.ds(c * CH, CH)] = rx_lo[0, pl.ds(c * CH, CH)]
        h0[pl.ds(HALO + ROWS + s * CH, CH)] = rx_hi[0, pl.ds(s * CH, CH)]

        def body0(k, carry, s=s):
            b = outward(s, k)
            cat, agg, pre, sig, act, xhat, inv, nxt = forward(0, b, h0)
            rows = pl.ds(b * BLK, RB * BLK)
            agg0[rows, :] = agg
            pre0[rows, :] = pre
            act0[rows, :] = act
            xh0[rows, :] = xhat
            inv0[rows, :] = inv
            h1[pl.ds(HALO + b, RB)] = nxt.reshape(RB, BLK, BLK)
            return carry

        lax.fori_loop(0, 2 * CH // RB, body0, 0)
        go(to_left(1, c, h1.at[pl.ds(HALO + c * CH, CH)]))
        go(to_right(1, s, h1.at[pl.ds(HALO + HALO + s * CH, CH)]))

    get_cot.wait()
    for s in range(NCH):
        c = NCH - 1 - s
        wait_low(1, c)
        wait_high(1, s)
        h1[pl.ds(c * CH, CH)] = rx_lo[1, pl.ds(c * CH, CH)]
        h1[pl.ds(HALO + ROWS + s * CH, CH)] = rx_hi[1, pl.ds(s * CH, CH)]

        def body1(k, carry, s=s):
            b = outward(s, k)
            cat, agg, pre, sig, act, xhat, inv, nxt = forward(1, b, h1)
            h2[pl.ds(b, RB)] = nxt.reshape(RB, BLK, BLK)
            g = cot[pl.ds(b, RB)].reshape(RB * BLK, BLK).astype(F32)
            backward(1, b, g, cat, pre, sig, act, xhat, inv)
            return carry

        lax.fori_loop(0, 2 * CH // RB, body1, 0)
    put_out = pltpu.make_async_copy(h2, out_feats, store_sem.at[0])
    put_out.start()

    def chain(seg, at, prev, value):
        seg[at] = value + jnp.where(prev >= 0, seg[jnp.maximum(prev, 0)], 0.0)

    def reach(s):
        def body(k, carry):
            t = s * CH + k
            chain(seg_a, t, tab[PREV_A + t], dot_tn(tiles[t, 1], gagg[t]))
            i = ROWS - 1 - t
            chain(seg_b, t, tab[PREV_B + t], dot_tn(tiles[i, 2], gagg[i]))
            return carry

        lax.fori_loop(0, CH, body, 0)

    def pick(seg, last):
        return jnp.where(last >= 0, seg[jnp.maximum(last, 0)], 0.0)

    def pack_low(y, c):
        def body(k, carry):
            out_lo[y, c * CH + k] = pick(seg_a, tab[LAST_A + c * CH + k]).astype(BF16)
            return carry

        lax.fori_loop(0, CH, body, 0)
        go(to_left(2 + y, c, out_lo.at[y, pl.ds(c * CH, CH)]))

    def pack_high(y, c):
        def body(k, carry):
            out_hi[y, c * CH + k] = pick(seg_b, tab[LAST_B + HALO + c * CH + k]).astype(BF16)
            return carry

        lax.fori_loop(0, CH, body, 0)
        go(to_right(2 + y, c, out_hi.at[y, pl.ds(c * CH, CH)]))

    def inside():
        def body(t, carry):
            chain(seg_c, t, tab[PREV_C + t], dot_tn(tiles[t, 2], gagg[t]))
            return carry

        lax.fori_loop(0, HALO, body, 0)

        def body2(t, carry):
            i = ROWS - 1 - t
            chain(seg_c, HALO + t, tab[PREV_C + HALO + t], dot_tn(tiles[i, 1], gagg[i]))
            return carry

        lax.fori_loop(0, HALO, body2, 0)

        def body3(j, carry):
            gacc[j] += (
                dot_tn(tiles[j, 0], gagg[j]) + pick(seg_c, tab[LAST_C + j]) + pick(seg_a, tab[LAST_A + HALO + j])
            )
            i = HALO + j
            gacc[i] += dot_tn(tiles[i, 0], gagg[i]) + pick(seg_c, tab[LAST_C + i]) + pick(seg_b, tab[LAST_B + j])
            return carry

        lax.fori_loop(0, HALO, body3, 0)

    def line_copy(layer, d):
        peer = lax.rem(line + d, LINE)
        return pltpu.make_async_remote_copy(
            src_ref=s1.at[layer, peer], dst_ref=r1.at[layer, d - 1], send_sem=s1_sem.at[layer, d - 1],
            recv_sem=r1_sem.at[layer, d - 1], device_id=on_line(peer), device_id_type=MESH,
        )

    def plane_copy(layer, d):
        return pltpu.make_async_remote_copy(
            src_ref=s2.at[layer], dst_ref=r2.at[layer, plane], send_sem=s2_sem.at[layer, d - 1],
            recv_sem=r2_sem.at[layer, d - 1], device_id=on_plane(lax.rem(plane + d, XZ)), device_id_type=MESH,
        )

    def gather_copy(layer, d):
        return pltpu.make_async_remote_copy(
            src_ref=s3.at[layer], dst_ref=r3.at[layer, line], send_sem=s3_sem.at[layer, d - 1],
            recv_sem=r3_sem.at[layer, d - 1], device_id=on_line(lax.rem(line + d, LINE)), device_id_type=MESH,
        )

    def reduce_line_start(layer):
        for p in range(LINE):
            s1[layer, p, pl.ds(0, WROWS), :] = acc_w[layer, pl.ds(p * WROWS, WROWS), :].astype(BF16)
            s1[layer, p, pl.ds(WROWS, 16), :] = acc_s[layer].astype(BF16)
        for d in range(1, LINE):
            line_copy(layer, d).start()

    def reduce_plane_start(layer):
        for d in range(1, LINE):
            line_copy(layer, d).wait()
        summed = s1[layer, line].astype(F32)
        for d in range(1, LINE):
            summed += r1[layer, d - 1].astype(F32)
        s2[layer] = summed.astype(BF16)
        r2[layer, plane] = summed.astype(BF16)
        for d in range(1, XZ):
            plane_copy(layer, d).start()

    def gather_start(layer):
        for d in range(1, XZ):
            plane_copy(layer, d).wait()
        summed = r2[layer, 0].astype(F32)
        for p in range(1, XZ):
            summed += r2[layer, p].astype(F32)
        s3[layer] = summed * scale
        r3[layer, line] = summed * scale
        for d in range(1, LINE):
            gather_copy(layer, d).start()

    def finish(layer):
        for d in range(1, LINE):
            gather_copy(layer, d).wait()
        for p in range(LINE):
            piece = r3[layer, p, pl.ds(0, WROWS), :]
            lo, hi = p * WROWS, (p + 1) * WROWS
            cut = min(max(256 - lo, 0), WROWS)
            if cut > 0:
                out_win[layer, pl.ds(lo, cut), :] = piece[:cut]
            if cut < WROWS:
                out_wout[layer, pl.ds(lo + cut - 256, WROWS - cut), :] = piece[cut:]
        out_bias[pl.ds(layer, 1), :] = r3[layer, 0, pl.ds(WROWS, 1), :]
        out_gain[pl.ds(layer, 1), :] = r3[layer, 0, pl.ds(WROWS + 1, 1), :]

    for s in range(NCH):
        reach(s)
    for s in range(NCH):
        pack_low(0, NCH - 1 - s)
        pack_high(0, s)
    reduce_line_start(1)
    inside()

    for s in range(NCH):
        c = NCH - 1 - s
        wait_low(2, s)
        wait_high(2, c)

        def body2(k, carry, s=s):
            b = inward(s, k)
            rows = pl.ds(b * BLK, RB * BLK)
            low = b < HALO
            at_lo = jnp.where(low, b, s * CH)
            at_hi = jnp.where(low, (NCH - 1 - s) * CH, b - HALO)
            come = jnp.where(low, rx_lo[2, pl.ds(at_lo, RB)], rx_hi[2, pl.ds(at_hi, RB)])
            g = (gacc[pl.ds(b, RB)] + come.astype(F32)).reshape(RB * BLK, BLK)
            cat = jnp.concatenate([h0[pl.ds(HALO + b, RB)].reshape(RB * BLK, BLK), agg0[rows, :]], axis=1)
            pre = pre0[rows, :]
            sig = 0.5 * jnp.tanh(0.5 * pre) + 0.5
            backward(0, b, g, cat, pre, sig, act0[rows, :], xh0[rows, :], inv0[rows, :])
            return carry

        lax.fori_loop(0, 2 * CH // RB, body2, 0)
        reach(s)
        pack_low(1, s)
        pack_high(1, c)
        if s == 0:
            reduce_plane_start(1)
        if s == 2:
            gather_start(1)
    reduce_line_start(0)
    inside()
    finish(1)
    reduce_plane_start(0)

    puts = []
    for s in range(NCH):
        c = NCH - 1 - s
        wait_low(3, c)
        wait_high(3, s)
        for b, rx, at in ((c * CH, rx_lo, c * CH), (HALO + s * CH, rx_hi, s * CH)):
            for k in range(CH):
                gacc[b + k] += rx[3, at + k].astype(F32)
            put = pltpu.make_async_copy(
                gacc.at[pl.ds(b, CH)], grad_feats.at[pl.ds(b, CH)], store_sem.at[1 + b // CH]
            )
            put.start()
            puts.append(put)
        if s == 2:
            gather_start(0)
    finish(0)
    put_out.wait()
    for put in puts:
        put.wait()
    for copy in sent:
        copy.wait_send()


def per_device(feats, tile_vals, tile_offs, w_in, bias_in, w_out, gain, cot):
    nodes, width = feats.shape
    total = nodes * lax.axis_size("band") * lax.axis_size("rep")
    scale = 1.0 / math.sqrt(total)
    smem = pl.BlockSpec(memory_space=pltpu.SMEM)
    vmem = pl.BlockSpec(memory_space=pltpu.VMEM)
    hbm = pl.BlockSpec(memory_space=pl.ANY)
    table = pl.pallas_call(
        links_kernel,
        out_shape=jax.ShapeDtypeStruct((TABLE,), jnp.int32),
        in_specs=[smem],
        out_specs=smem,
    )(tile_offs)

    blocks = (ROWS, BLK, width)
    ext = (ROWS + 2 * HALO, BLK, width)
    dma = pltpu.SemaphoreType.DMA
    outs = pl.pallas_call(
        functools.partial(main_kernel, scale),
        out_shape=(
            jax.ShapeDtypeStruct(blocks, BF16),
            jax.ShapeDtypeStruct(blocks, F32),
            jax.ShapeDtypeStruct(w_in.shape, F32),
            jax.ShapeDtypeStruct(bias_in.shape, F32),
            jax.ShapeDtypeStruct(w_out.shape, F32),
            jax.ShapeDtypeStruct(gain.shape, F32),
        ),
        in_specs=[hbm, hbm, hbm, smem, vmem, vmem, vmem, vmem],
        out_specs=(hbm, hbm, vmem, vmem, vmem, vmem),
        scratch_shapes=[
            pltpu.VMEM(tile_vals.shape, BF16),
            pltpu.VMEM(ext, BF16),
            pltpu.VMEM(ext, BF16),
            pltpu.VMEM(blocks, BF16),
            pltpu.VMEM(blocks, BF16),
            pltpu.VMEM((nodes, width), BF16),
            pltpu.VMEM((nodes, width), F32),
            pltpu.VMEM((nodes, width), BF16),
            pltpu.VMEM((nodes, width), F32),
            pltpu.VMEM((nodes, 1), F32),
            pltpu.VMEM(blocks, F32),
            pltpu.VMEM(blocks, BF16),
            pltpu.VMEM((HALO, BLK, width), F32),
            pltpu.VMEM((HALO, BLK, width), F32),
            pltpu.VMEM((ROWS, BLK, width), F32),
            pltpu.VMEM((2, HALO, BLK, width), BF16),
            pltpu.VMEM((2, HALO, BLK, width), BF16),
            pltpu.VMEM((4, HALO, BLK, width), BF16),
            pltpu.VMEM((4, HALO, BLK, width), BF16),
            pltpu.VMEM((2, 384, 128), F32),
            pltpu.VMEM((2, 16, 128), F32),
            pltpu.VMEM((2, LINE, PIECE, 128), BF16),
            pltpu.VMEM((2, LINE - 1, PIECE, 128), BF16),
            pltpu.VMEM((2, PIECE, 128), BF16),
            pltpu.VMEM((2, XZ, PIECE, 128), BF16),
            pltpu.VMEM((2, PIECE, 128), F32),
            pltpu.VMEM((2, LINE, PIECE, 128), F32),
            dma((3,)),
            dma((9,)),
            dma((4, NCH)),
            dma((4, NCH)),
            dma((4, NCH)),
            dma((4, NCH)),
            dma((2, LINE - 1)),
            dma((2, LINE - 1)),
            dma((2, XZ - 1)),
            dma((2, XZ - 1)),
            dma((2, LINE - 1)),
            dma((2, LINE - 1)),
        ],
        compiler_params=pltpu.CompilerParams(
            collective_id=0, has_side_effects=True, vmem_limit_bytes=56 * 2**20
        ),
        cost_estimate=pl.CostEstimate(flops=4 * 10**9, bytes_accessed=9 * 10**6, transcendentals=10**6),
    )(feats.reshape(blocks), tile_vals, cot.reshape(blocks), table, w_in, bias_in, w_out, gain)
    return (outs[0].reshape(feats.shape), outs[1].reshape(feats.shape), *outs[2:])


def solution(mesh):
    rows = P(("band", "rep"), None)
    placed = (rows, P(("band", "rep"), None, None, None), rows, P(), P(), P(), P(), rows)
    return jax.shard_map(
        per_device,
        mesh=mesh,
        in_specs=placed,
        out_specs=(rows, rows, P(), P(), P(), P()),
        check_vma=False,
    )
```

time: 357 us -> 112 us (0.31)
  waiting for transfers between devices: 106 us -> 0 us
  Pallas kernels: 0 us -> 103 us
  local copies, waits for them, and re-layouts: 84.6 us -> 7.6 us
  other arithmetic: 76.5 us -> 0 us
  matrix products: 41.4 us -> 0 us
  starting transfers between devices: 32 us -> 0 us
  between operations: 14.5 us -> 0.67 us
    pallas_call x0 -> x2, Pallas kernels: none -> 103 us  [the longest x1 101 us: per_device(): pl.pallas_call(functools.partial(main_kernel, scale), out_shape=(jax.Shap...]
    psum x1 -> x0, waiting for transfers between devices: 102 us -> none  [packed_total(): subtotal = lax.psum(jnp.concatenate([a.ravel() for a in arrays]), axis)]
    scatter-add x6 -> x0, other arithmetic: 54.2 us -> none  [the longest x2 40 us: per_device(): extended.at[flat_columns].add(contrib.reshape(-1, tile_width, feat_width))]
    dot_general x20 -> x0, matrix products: 41.4 us -> none  [the longest x2 7.38 us: per_device(): jnp.einsum('bkij,bid->bkjd', tile_vals, grad_blocks, preferred_element_ty...]
    ppermute x12 -> x0, starting transfers between devices: 32 us -> none  [from_behind(): return lax.ppermute(x, axis, [(i, (i + by) % peers) for i in range(peers)])]
    slice x12 -> x0, local copies, waits for them, and re-layouts: 22.9 us -> none  [the longest x4 12.3 us: per_device(): extended.reshape(-1, feat_width)[rim_rows:rim_rows + node_rows]]
    reshape x5 -> x0, local copies, waits for them, and re-layouts: 19.6 us -> none  [the longest x2 13.2 us: per_device(): contrib.reshape(-1, tile_width, feat_width)]
    unnamed x66 -> x17, local copies, waits for them, and re-layouts: 19.8 us -> 7.6 us
  transfers between devices with their start and end apart: 13 -> 0, of which waited for: 4 -> 0; matrix products, arithmetic and copies ran while one was open for 40% -> 0% of each run, Pallas kernels for 0% -> 0%
where the time goes in v1:
time: 112 us
  Pallas kernels  103 us (92%)
  local copies, waits for them, and re-layouts  7.6 us (7%)
    pallas_call x1, Pallas kernels, per_device(): pl.pallas_call(functools.partial(main_kernel, scale), out_shape=(jax.Shap...  101 us
    unnamed x17, local copies, waits for them, and re-layouts  7.6 us
    pallas_call x1, Pallas kernels, per_device(): pl.pallas_call(links_kernel, out_shape=jax.ShapeDtypeStruct((TABLE,), jnp...  2.66 us

profile of v1, /device:TPU:1, one launch (start us, length us, event | category | flops | bytes accessed | tf_op | source)
XLA Modules:
  0.0 111.7 jit_solution(1090779777331433902)
XLA Ops:
  0.6 1.4 %copy.14.offs = s32[32,3]{1,0:T(8,128)} copy(s32[32,3]{0,1:T(4,128)} %param.10) | data formatting | bytes 768 | tf_op args[2]
  2.0 2.7 %shard_map.127.tab = s32[224]{0:T(256)} custom-call(s32[32,3]{1,0:T(8,128)} %copy.14.offs), custom_call_target="tpu_custom_call" | custom-call | tf_op jit(solution)/shard_map/pallas_call | solution.py:441
  4.7 100.7 %shard_map.128 = (bf16[32,128,128]{2,1,0:T(8,128)(2,1)}, f32[32,128,128]{2,1,0:T(8,128)}, f32[2,256,128]{2,1,0:T(8,128)}, f32[2,128]{1,0:T(2,128)}, f32[2,128,128]{2,1,0:T(8,128)}, /*index=5*/f32[2,128]{1,0:T(2,128)}) custom-call(bf16[32,128,128]{2,1,0:T(8,128)(2,1)} %bitcast.6, bf16[32,3,128,128]{3,2,1,0:T(8,128)(2,1)} %tiles_in.1, ...), custom_call_target="tpu_custom_call" | custom-call | flops 4000000000 | bytes 9000000 | tf_op jit(solution)/shard_map/pallas_call | solution.py:451
  105.4 0.0 copy-start
  105.4 2.4 %copy.21 = bf16[4096,128]{1,0:T(8,128)(2,1)} copy(bf16[4096,128]{1,0:T(8,128)(2,1)} %bitcast.5) | data formatting | bytes 2097152
  107.8 0.0 copy-done
  107.8 0.0 copy-start.1
  107.8 0.0 copy-start.4
  107.8 0.0 copy-start.2
  107.8 0.0 copy-start.3
  107.9 1.3 %copy.22 = f32[4096,128]{1,0:T(8,128)} copy(f32[4096,128]{1,0:T(8,128)S(1)} %bitcast.4) | data formatting | bytes 4194304
  109.2 0.0 copy-done.1
  109.2 0.7 copy.23
  109.9 0.0 copy-done.4
  109.9 0.6 copy.24
  110.4 0.0 copy-done.2
  110.5 0.7 copy.25
  111.1 0.0 copy-done.3
  111.1 0.6 copy.26
Async XLA Ops:
  105.4 2.4 %copy-start = (f32[32,128,128]{2,1,0:T(8,128)S(1)}, f32[32,128,128]{2,1,0:T(8,128)}, u32[]{:S(2)}) copy-start(f32[32,128,128]{2,1,0:T(8,128)} %get-tuple-element.13) | copy-start | bytes 6291460
  107.8 1.3 %copy-start.1 = (f32[2,256,128]{2,1,0:T(8,128)S(1)}, f32[2,256,128]{2,1,0:T(8,128)}, u32[]{:S(2)}) copy-start(f32[2,256,128]{2,1,0:T(8,128)} %get-tuple-element.26) | copy-start | bytes 786436
  107.8 2.0 %copy-start.4 = (f32[2,128]{1,0:T(2,128)S(1)}, f32[2,128]{1,0:T(2,128)}, u32[]{:S(2)}) copy-start(f32[2,128]{1,0:T(2,128)} %get-tuple-element.27) | copy-start | bytes 3076
  107.8 2.6 %copy-start.2 = (f32[2,128,128]{2,1,0:T(8,128)S(1)}, f32[2,128,128]{2,1,0:T(8,128)}, u32[]{:S(2)}) copy-start(f32[2,128,128]{2,1,0:T(8,128)} %get-tuple-element.28) | copy-start | bytes 393220
  107.8 3.3 %copy-start.3 = (f32[2,128]{1,0:T(2,128)S(1)}, f32[2,128]{1,0:T(2,128)}, u32[]{:S(2)}) copy-start(f32[2,128]{1,0:T(2,128)} %get-tuple-element.29) | copy-start | bytes 3076

commit v2 on v1

--- a/solution.py
+++ b/solution.py
@@ -14,7 +14,8 @@
 BLK = 128
 CH = 4
 NCH = HALO // CH
-RB = 2
+EARLY = 1
+RB = 4
 XZ = 16
 LINE = 8
 PIECE = 64
@@ -22,45 +23,41 @@
 F32 = jnp.float32
 BF16 = jnp.bfloat16
 
-COL1, COL2 = 0, 32
-PREV_A, PREV_B, PREV_C = 64, 80, 96
-LAST_A, LAST_B, LAST_C = 128, 160, 192
+PREV_A, PREV_B, PREV_C = 0, 16, 32
+LAST_A, LAST_B, LAST_C = 64, 96, 128
+COLS_A, COLS_B, COLS_C = 160, 176, 192
 TABLE = 224
 
 
-def links_kernel(offs, tab):
-    def clear(k, carry):
-        tab[LAST_A + k] = -1
+def links(offs, tab):
+    def columns(t, carry):
+        i = ROWS - 1 - t
+        tab[COLS_A + t] = HALO + t + offs[1, t]
+        tab[COLS_B + t] = i - HALO + offs[2, i]
+        tab[COLS_C + t] = t + offs[2, t]
+        tab[COLS_C + HALO + t] = i + offs[1, i]
         return carry
 
-    lax.fori_loop(0, 96, clear, 0)
-
-    def low(i, carry):
-        col = HALO + i + offs[i, 1]
-        tab[COL1 + i] = col
-        tab[PREV_A + i] = tab[LAST_A + col]
-        tab[LAST_A + col] = i
-        col = i + offs[i, 2]
-        tab[COL2 + i] = HALO + col
-        tab[PREV_C + i] = tab[LAST_C + col]
-        tab[LAST_C + col] = i
-        return carry
-
-    lax.fori_loop(0, HALO, low, 0)
-
-    def high(t, carry):
-        i = ROWS - 1 - t
-        col = i - HALO + offs[i, 2]
-        tab[COL2 + i] = 2 * HALO + col
-        tab[PREV_B + t] = tab[LAST_B + col]
-        tab[LAST_B + col] = t
-        col = i + offs[i, 1]
-        tab[COL1 + i] = HALO + col
-        tab[PREV_C + HALO + t] = tab[LAST_C + col]
-        tab[LAST_C + col] = HALO + t
-        return carry
-
-    lax.fori_loop(0, HALO, high, 0)
+    lax.fori_loop(0, HALO, columns, 0)
+    for cols, prev, last, count in (
+        (COLS_A, PREV_A, LAST_A, HALO), (COLS_B, PREV_B, LAST_B, HALO), (COLS_C, PREV_C, LAST_C, 2 * HALO)
+    ):
+        def find_prev(e, carry, cols=cols, prev=prev, count=count):
+            col, found = tab[cols + e], jnp.int32(-1)
+            for k in range(count):
+                found = jnp.where((tab[cols + k] == col) & (k < e), k, found)
+            tab[prev + e] = found
+            return carry
+
+        def find_last(c, carry, cols=cols, last=last, count=count):
+            found = jnp.int32(-1)
+            for k in range(count):
+                found = jnp.where(tab[cols + k] == c, k, found)
+            tab[last + c] = found
+            return carry
+
+        lax.fori_loop(0, count, find_prev, 0)
+        lax.fori_loop(0, ROWS, find_last, 0)
 
 
 def dot(a, b):
@@ -77,12 +74,12 @@
 
 def main_kernel(
     scale,
-    feats, tiles_in, cot_in, tab, w_in, bias, w_out, gain,
-    out_feats, grad_feats, out_win, out_bias, out_wout, out_gain,
-    tiles, h0, h1, h2, cot, agg0, pre0, act0, xh0, inv0, gacc, gagg,
+    feats, tiles_in, cot_in, offs, w_in, bias, w_out, gain,
+    h2, gacc, out_win, out_bias, out_wout, out_gain,
+    tab, tiles, h0, h1, cot, agg0, pre0, act0, xh0, inv0, gagg,
     seg_a, seg_b, seg_c, out_lo, out_hi, rx_lo, rx_hi, acc_w, acc_s,
     s1, r1, s2, r2, s3, r3,
-    local_sem, store_sem, tx_lo_sem, tx_hi_sem, rx_lo_sem, rx_hi_sem,
+    local_sem, tx_lo_sem, tx_hi_sem, rx_lo_sem, rx_hi_sem,
     s1_sem, r1_sem, s2_sem, r2_sem, s3_sem, r3_sem,
 ):
     band, rep = lax.axis_index("band"), lax.axis_index("rep")
@@ -95,14 +92,19 @@
 
     left = place(lax.rem(me + total - 1, total))
     right = place(lax.rem(me + 1, total))
-    y_hi, plane = lax.div(band, XZ), lax.rem(band, XZ)
-    line = y_hi * n_rep + rep
+    y_hi, x, z = lax.div(band, 16), lax.rem(lax.div(band, 4), 4), lax.rem(band, 4)
+    y_lo, core = lax.div(rep, 2), lax.rem(rep, 2)
+    line = x * 2 + core
+    plane = z * 4 + y_hi * 2 + y_lo
 
     def on_line(index):
-        return (lax.div(index, n_rep) * XZ + plane, lax.rem(index, n_rep))
+        return (y_hi * 16 + lax.div(index, 2) * 4 + z, y_lo * 2 + lax.rem(index, 2))
 
     def on_plane(index):
-        return (y_hi * XZ + index, rep)
+        return (
+            lax.rem(lax.div(index, 2), 2) * 16 + x * 4 + lax.div(index, 4),
+            lax.rem(index, 2) * 2 + core,
+        )
 
     barrier = pltpu.get_barrier_semaphore()
     for peer in (left, right):
@@ -152,6 +154,7 @@
         c = NCH - 1 - s
         go(to_left(0, s, feats.at[pl.ds(s * CH, CH)]))
         go(to_right(0, c, feats.at[pl.ds(HALO + c * CH, CH)]))
+    links(offs, tab)
     get_feats.wait()
     get_tiles.wait()
 
@@ -161,8 +164,8 @@
         for r in range(RB):
             tile = tiles[b + r]
             lhs = jnp.concatenate([tile[0], tile[1]], axis=1)
-            rhs = jnp.concatenate([own[r], ext[tab[COL1 + b + r]]], axis=0)
-            sums.append((dot(lhs, rhs) + dot(tile[2], ext[tab[COL2 + b + r]])).astype(BF16))
+            rhs = jnp.concatenate([own[r], ext[HALO + b + r + offs[1, b + r]]], axis=0)
+            sums.append((dot(lhs, rhs) + dot(tile[2], ext[HALO + b + r + offs[2, b + r]])).astype(BF16))
         own = own.reshape(RB * BLK, BLK)
         agg = jnp.concatenate(sums, axis=0)
         cat = jnp.concatenate([own, agg], axis=1)
@@ -226,9 +229,11 @@
             h1[pl.ds(HALO + b, RB)] = nxt.reshape(RB, BLK, BLK)
             return carry
 
-        lax.fori_loop(0, 2 * CH // RB, body0, 0)
-        go(to_left(1, c, h1.at[pl.ds(HALO + c * CH, CH)]))
-        go(to_right(1, s, h1.at[pl.ds(HALO + HALO + s * CH, CH)]))
+        lax.fori_loop(0, 2 * CH // RB, body0, 0, unroll=2)
+        for late in (s,) if s < EARLY else range(NCH - 1, EARLY - 1, -1) if s == NCH - 1 else ():
+            c = NCH - 1 - late
+            go(to_left(1, c, h1.at[pl.ds(HALO + c * CH, CH)]))
+            go(to_right(1, late, h1.at[pl.ds(HALO + HALO + late * CH, CH)]))
 
     get_cot.wait()
     for s in range(NCH):
@@ -246,9 +251,7 @@
             backward(1, b, g, cat, pre, sig, act, xhat, inv)
             return carry
 
-        lax.fori_loop(0, 2 * CH // RB, body1, 0)
-    put_out = pltpu.make_async_copy(h2, out_feats, store_sem.at[0])
-    put_out.start()
+        lax.fori_loop(0, 2 * CH // RB, body1, 0, unroll=2)
 
     def chain(seg, at, prev, value):
         seg[at] = value + jnp.where(prev >= 0, seg[jnp.maximum(prev, 0)], 0.0)
@@ -261,7 +264,7 @@
             chain(seg_b, t, tab[PREV_B + t], dot_tn(tiles[i, 2], gagg[i]))
             return carry
 
-        lax.fori_loop(0, CH, body, 0)
+        lax.fori_loop(0, CH, body, 0, unroll=4)
 
     def pick(seg, last):
         return jnp.where(last >= 0, seg[jnp.maximum(last, 0)], 0.0)
@@ -271,7 +274,7 @@
             out_lo[y, c * CH + k] = pick(seg_a, tab[LAST_A + c * CH + k]).astype(BF16)
             return carry
 
-        lax.fori_loop(0, CH, body, 0)
+        lax.fori_loop(0, CH, body, 0, unroll=4)
         go(to_left(2 + y, c, out_lo.at[y, pl.ds(c * CH, CH)]))
 
     def pack_high(y, c):
@@ -279,7 +282,7 @@
             out_hi[y, c * CH + k] = pick(seg_b, tab[LAST_B + HALO + c * CH + k]).astype(BF16)
             return carry
 
-        lax.fori_loop(0, CH, body, 0)
+        lax.fori_loop(0, CH, body, 0, unroll=4)
         go(to_right(2 + y, c, out_hi.at[y, pl.ds(c * CH, CH)]))
 
     def inside():
@@ -287,14 +290,14 @@
             chain(seg_c, t, tab[PREV_C + t], dot_tn(tiles[t, 2], gagg[t]))
             return carry
 
-        lax.fori_loop(0, HALO, body, 0)
+        lax.fori_loop(0, HALO, body, 0, unroll=16)
 
         def body2(t, carry):
             i = ROWS - 1 - t
             chain(seg_c, HALO + t, tab[PREV_C + HALO + t], dot_tn(tiles[i, 1], gagg[i]))
             return carry
 
-        lax.fori_loop(0, HALO, body2, 0)
+        lax.fori_loop(0, HALO, body2, 0, unroll=16)
 
         def body3(j, carry):
             gacc[j] += (
@@ -304,7 +307,7 @@
             gacc[i] += dot_tn(tiles[i, 0], gagg[i]) + pick(seg_c, tab[LAST_C + i]) + pick(seg_b, tab[LAST_B + j])
             return carry
 
-        lax.fori_loop(0, HALO, body3, 0)
+        lax.fori_loop(0, HALO, body3, 0, unroll=16)
 
     def line_copy(layer, d):
         peer = lax.rem(line + d, LINE)
@@ -395,7 +398,7 @@
             backward(0, b, g, cat, pre, sig, act0[rows, :], xh0[rows, :], inv0[rows, :])
             return carry
 
-        lax.fori_loop(0, 2 * CH // RB, body2, 0)
+        lax.fori_loop(0, 2 * CH // RB, body2, 0, unroll=2)
         reach(s)
         pack_low(1, s)
         pack_high(1, c)
@@ -408,7 +411,6 @@
     finish(1)
     reduce_plane_start(0)
 
-    puts = []
     for s in range(NCH):
         c = NCH - 1 - s
         wait_low(3, c)
@@ -416,19 +418,20 @@
         for b, rx, at in ((c * CH, rx_lo, c * CH), (HALO + s * CH, rx_hi, s * CH)):
             for k in range(CH):
                 gacc[b + k] += rx[3, at + k].astype(F32)
-            put = pltpu.make_async_copy(
-                gacc.at[pl.ds(b, CH)], grad_feats.at[pl.ds(b, CH)], store_sem.at[1 + b // CH]
-            )
-            put.start()
-            puts.append(put)
         if s == 2:
             gather_start(0)
     finish(0)
-    put_out.wait()
-    for put in puts:
-        put.wait()
     for copy in sent:
         copy.wait_send()
+
+
+def publish_kernel(*refs):
+    sem = refs[12]
+    copies = [pltpu.make_async_copy(refs[k], refs[6 + k], sem.at[k]) for k in range(6)]
+    for copy in copies:
+        copy.start()
+    for copy in copies:
+        copy.wait()
 
 
 def per_device(feats, tile_vals, tile_offs, w_in, bias_in, w_out, gain, cot):
@@ -438,40 +441,32 @@
     smem = pl.BlockSpec(memory_space=pltpu.SMEM)
     vmem = pl.BlockSpec(memory_space=pltpu.VMEM)
     hbm = pl.BlockSpec(memory_space=pl.ANY)
-    table = pl.pallas_call(
-        links_kernel,
-        out_shape=jax.ShapeDtypeStruct((TABLE,), jnp.int32),
-        in_specs=[smem],
-        out_specs=smem,
-    )(tile_offs)
-
     blocks = (ROWS, BLK, width)
     ext = (ROWS + 2 * HALO, BLK, width)
     dma = pltpu.SemaphoreType.DMA
     outs = pl.pallas_call(
         functools.partial(main_kernel, scale),
         out_shape=(
-            jax.ShapeDtypeStruct(blocks, BF16),
-            jax.ShapeDtypeStruct(blocks, F32),
-            jax.ShapeDtypeStruct(w_in.shape, F32),
-            jax.ShapeDtypeStruct(bias_in.shape, F32),
-            jax.ShapeDtypeStruct(w_out.shape, F32),
-            jax.ShapeDtypeStruct(gain.shape, F32),
+            pltpu.VMEM(blocks, BF16),
+            pltpu.VMEM(blocks, F32),
+            pltpu.VMEM(w_in.shape, F32),
+            pltpu.VMEM(bias_in.shape, F32),
+            pltpu.VMEM(w_out.shape, F32),
+            pltpu.VMEM(gain.shape, F32),
         ),
         in_specs=[hbm, hbm, hbm, smem, vmem, vmem, vmem, vmem],
-        out_specs=(hbm, hbm, vmem, vmem, vmem, vmem),
+        out_specs=(vmem,) * 6,
         scratch_shapes=[
+            pltpu.SMEM((TABLE,), jnp.int32),
             pltpu.VMEM(tile_vals.shape, BF16),
             pltpu.VMEM(ext, BF16),
             pltpu.VMEM(ext, BF16),
-            pltpu.VMEM(blocks, BF16),
             pltpu.VMEM(blocks, BF16),
             pltpu.VMEM((nodes, width), BF16),
             pltpu.VMEM((nodes, width), F32),
             pltpu.VMEM((nodes, width), BF16),
             pltpu.VMEM((nodes, width), F32),
             pltpu.VMEM((nodes, 1), F32),
-            pltpu.VMEM(blocks, F32),
             pltpu.VMEM(blocks, BF16),
             pltpu.VMEM((HALO, BLK, width), F32),
             pltpu.VMEM((HALO, BLK, width), F32),
@@ -489,7 +484,6 @@
             pltpu.VMEM((2, PIECE, 128), F32),
             pltpu.VMEM((2, LINE, PIECE, 128), F32),
             dma((3,)),
-            dma((9,)),
             dma((4, NCH)),
             dma((4, NCH)),
             dma((4, NCH)),
@@ -505,8 +499,16 @@
             collective_id=0, has_side_effects=True, vmem_limit_bytes=56 * 2**20
         ),
         cost_estimate=pl.CostEstimate(flops=4 * 10**9, bytes_accessed=9 * 10**6, transcendentals=10**6),
-    )(feats.reshape(blocks), tile_vals, cot.reshape(blocks), table, w_in, bias_in, w_out, gain)
-    return (outs[0].reshape(feats.shape), outs[1].reshape(feats.shape), *outs[2:])
+    )(feats.reshape(blocks), tile_vals, cot.reshape(blocks), tile_offs.T, w_in, bias_in, w_out, gain)
+    outs = (outs[0].reshape(feats.shape), outs[1].reshape(feats.shape), *outs[2:])
+    return pl.pallas_call(
+        publish_kernel,
+        out_shape=tuple(jax.ShapeDtypeStruct(o.shape, o.dtype) for o in outs),
+        in_specs=[hbm] * 6,
+        out_specs=(hbm,) * 6,
+        scratch_shapes=[dma((6,))],
+        compiler_params=pltpu.CompilerParams(vmem_limit_bytes=2**20),
+    )(*outs)
 
 
 def solution(mesh):

time: 112 us -> 82.7 us (0.74)
  Pallas kernels: 103 us -> 81.7 us
  local copies, waits for them, and re-layouts: 7.6 us -> 0 us
    pallas_call x2, Pallas kernels: 103 us -> 81.7 us  [the longest x1 79.9 us: per_device(): pl.pallas_call(functools.partial(main_kernel, scale), out_shape=(pltpu.VM...]
    unnamed x17 -> x0, local copies, waits for them, and re-layouts: 7.6 us -> none
where the time goes in v2:
time: 82.7 us; the launch traced here: 82.5 us
  Pallas kernels  81.7 us (99%)
    pallas_call x1, Pallas kernels, per_device(): pl.pallas_call(functools.partial(main_kernel, scale), out_shape=(pltpu.VM...  79.9 us
    pallas_call x1, Pallas kernels, per_device(): pl.pallas_call(publish_kernel, out_shape=tuple((jax.ShapeDtypeStruct(o.sh...  1.84 us

profile of v2, /device:TPU:1, one launch (start us, length us, event | category | flops | bytes accessed | tf_op | source)
XLA Modules:
  0.0 82.5 jit_solution(12377586923415074959)
XLA Ops:
  0.6 79.9 %shard_map.127 = (bf16[32,128,128]{2,1,0:T(8,128)(2,1)S(1)}, f32[32,128,128]{2,1,0:T(8,128)S(1)}, f32[2,256,128]{2,1,0:T(8,128)S(1)}, f32[2,128]{1,0:T(2,128)S(1...) custom-call(bf16[32,128,128]{2,1,0:T(8,128)(2,1)} %bitcast.7, bf16[32,3,128,128]{3,2,1,0:T(8,128)(2,1)} %tiles_in.1, ...), custom_call_target="tpu_custom_call" | custom-call | flops 4000000000 | bytes 9000000 | tf_op jit(solution)/shard_map/pallas_call | solution.py:447
  80.5 1.8 %shard_map.128 = (bf16[4096,128]{1,0:T(8,128)(2,1)}, f32[4096,128]{1,0:T(8,128)}, f32[2,256,128]{2,1,0:T(8,128)}, f32[2,128]{1,0:T(2,128)}, f32[2,128,128]{2,1,0:T(8,128)}, /*index=5*/f32[2,128]{1,0:T(2,128)}) custom-call(bf16[4096,128]{1,0:T(8,128)(2,1)S(1)} %bitcast.6, f32[4096,128]{1,0:T(8,128)S(1)} %bitcast.5, ...), custom_call_target="tpu_custom_call" | custom-call | tf_op jit(solution)/shard_map/pallas_call | solution.py:504

commit v3 on v2

--- a/solution.py
+++ b/solution.py
@@ -15,6 +15,7 @@
 CH = 4
 NCH = HALO // CH
 EARLY = 1
+EARLY_BACK = 0
 RB = 4
 XZ = 16
 LINE = 8
@@ -143,6 +144,19 @@
         copy.start()
         sent.append(copy)
         return copy
+
+    held = []
+
+    def hold(copy):
+        held.append(copy)
+
+    def release(before=()):
+        for copy in before:
+            copy.wait_send()
+            sent[:] = [k for k in sent if k is not copy]
+        for copy in (held.pop(0), held.pop(0)):
+            go(copy)
+        return tuple(sent[-2:])
 
     def wait_low(x, c):
         to_right(x, c, rx_lo.at[x, pl.ds(c * CH, CH)]).wait_recv()
@@ -232,12 +246,18 @@
         lax.fori_loop(0, 2 * CH // RB, body0, 0, unroll=2)
         for late in (s,) if s < EARLY else range(NCH - 1, EARLY - 1, -1) if s == NCH - 1 else ():
             c = NCH - 1 - late
-            go(to_left(1, c, h1.at[pl.ds(HALO + c * CH, CH)]))
-            go(to_right(1, late, h1.at[pl.ds(HALO + HALO + late * CH, CH)]))
+            hold(to_left(1, c, h1.at[pl.ds(HALO + c * CH, CH)]))
+            hold(to_right(1, late, h1.at[pl.ds(HALO + HALO + late * CH, CH)]))
+        if s < EARLY:
+            release()
+    first = release()
+    second = release()
 
     get_cot.wait()
     for s in range(NCH):
         c = NCH - 1 - s
+        if s == 0:
+            release(first)
         wait_low(1, c)
         wait_high(1, s)
         h1[pl.ds(c * CH, CH)] = rx_lo[1, pl.ds(c * CH, CH)]
@@ -275,7 +295,7 @@
             return carry
 
         lax.fori_loop(0, CH, body, 0, unroll=4)
-        go(to_left(2 + y, c, out_lo.at[y, pl.ds(c * CH, CH)]))
+        hold(to_left(2 + y, c, out_lo.at[y, pl.ds(c * CH, CH)]))
 
     def pack_high(y, c):
         def body(k, carry):
@@ -283,7 +303,7 @@
             return carry
 
         lax.fori_loop(0, CH, body, 0, unroll=4)
-        go(to_right(2 + y, c, out_hi.at[y, pl.ds(c * CH, CH)]))
+        hold(to_right(2 + y, c, out_hi.at[y, pl.ds(c * CH, CH)]))
 
     def inside():
         def body(t, carry):
@@ -352,8 +372,9 @@
         summed = r2[layer, 0].astype(F32)
         for p in range(1, XZ):
             summed += r2[layer, p].astype(F32)
-        s3[layer] = summed * scale
-        r3[layer, line] = summed * scale
+        summed = (summed * scale).astype(BF16)
+        s3[layer] = summed
+        r3[layer, line] = summed
         for d in range(1, LINE):
             gather_copy(layer, d).start()
 
@@ -361,26 +382,32 @@
         for d in range(1, LINE):
             gather_copy(layer, d).wait()
         for p in range(LINE):
-            piece = r3[layer, p, pl.ds(0, WROWS), :]
+            piece = r3[layer, p, pl.ds(0, WROWS), :].astype(F32)
             lo, hi = p * WROWS, (p + 1) * WROWS
             cut = min(max(256 - lo, 0), WROWS)
             if cut > 0:
                 out_win[layer, pl.ds(lo, cut), :] = piece[:cut]
             if cut < WROWS:
                 out_wout[layer, pl.ds(lo + cut - 256, WROWS - cut), :] = piece[cut:]
-        out_bias[pl.ds(layer, 1), :] = r3[layer, 0, pl.ds(WROWS, 1), :]
-        out_gain[pl.ds(layer, 1), :] = r3[layer, 0, pl.ds(WROWS + 1, 1), :]
+        small = r3[layer, 0, pl.ds(WROWS, 16), :].astype(F32)
+        out_bias[pl.ds(layer, 1), :] = small[:1]
+        out_gain[pl.ds(layer, 1), :] = small[1:2]
 
     for s in range(NCH):
         reach(s)
     for s in range(NCH):
         pack_low(0, NCH - 1 - s)
         pack_high(0, s)
+        if s < 2:
+            ahead = (*ahead, release()) if s else (release(),)
     reduce_line_start(1)
     inside()
+    release(ahead[0])
 
     for s in range(NCH):
         c = NCH - 1 - s
+        if s == 0:
+            release(ahead[1])
         wait_low(2, s)
         wait_high(2, c)
 
@@ -400,16 +427,25 @@
 
         lax.fori_loop(0, 2 * CH // RB, body2, 0, unroll=2)
         reach(s)
+        if s < EARLY_BACK:
+            pack_low(1, s)
+            pack_high(1, c)
+            release()
+        if s == 2:
+            reduce_plane_start(1)
+    reduce_line_start(0)
+    for s in range(EARLY_BACK, NCH):
         pack_low(1, s)
-        pack_high(1, c)
-        if s == 0:
-            reduce_plane_start(1)
-        if s == 2:
-            gather_start(1)
-    reduce_line_start(0)
+        pack_high(1, NCH - 1 - s)
+        if s < EARLY_BACK + 2:
+            ahead = (*ahead, release()) if s > EARLY_BACK else (release(),)
+    gather_start(1)
     inside()
+    reduce_plane_start(0)
+    release(ahead[0])
+    while held:
+        ahead = (ahead[1], release(ahead[1]))
     finish(1)
-    reduce_plane_start(0)
 
     for s in range(NCH):
         c = NCH - 1 - s
@@ -418,7 +454,7 @@
         for b, rx, at in ((c * CH, rx_lo, c * CH), (HALO + s * CH, rx_hi, s * CH)):
             for k in range(CH):
                 gacc[b + k] += rx[3, at + k].astype(F32)
-        if s == 2:
+        if s == 1:
             gather_start(0)
     finish(0)
     for copy in sent:
@@ -481,8 +517,8 @@
             pltpu.VMEM((2, LINE - 1, PIECE, 128), BF16),
             pltpu.VMEM((2, PIECE, 128), BF16),
             pltpu.VMEM((2, XZ, PIECE, 128), BF16),
-            pltpu.VMEM((2, PIECE, 128), F32),
-            pltpu.VMEM((2, LINE, PIECE, 128), F32),
+            pltpu.VMEM((2, PIECE, 128), BF16),
+            pltpu.VMEM((2, LINE, PIECE, 128), BF16),
             dma((3,)),
             dma((4, NCH)),
             dma((4, NCH)),

time: 82.7 us -> 79.1 us (0.956)
  Pallas kernels: 81.7 us -> 78.2 us
    pallas_call x1, Pallas kernels: 79.9 us -> 76.4 us  [per_device(): pl.pallas_call(functools.partial(main_kernel, scale), out_shape=(pltpu.VM...]
where the time goes in v3:
time: 79.1 us; the launch traced here: 79 us
  Pallas kernels  78.2 us (99%)
  between operations  0.8 us (1%)
    pallas_call x1, Pallas kernels, per_device(): pl.pallas_call(functools.partial(main_kernel, scale), out_shape=(pltpu.VM...  76.4 us
    pallas_call x1, Pallas kernels, per_device(): pl.pallas_call(publish_kernel, out_shape=tuple((jax.ShapeDtypeStruct(o.sh...  1.84 us

profile of v3, /device:TPU:1, one launch (start us, length us, event | category | flops | bytes accessed | tf_op | source)
XLA Modules:
  0.0 79.0 jit_solution(5030670444918386353)
XLA Ops:
  0.6 76.4 %shard_map.127 = (bf16[32,128,128]{2,1,0:T(8,128)(2,1)S(1)}, f32[32,128,128]{2,1,0:T(8,128)S(1)}, f32[2,256,128]{2,1,0:T(8,128)S(1)}, f32[2,128]{1,0:T(2,128)S(1...) custom-call(bf16[32,128,128]{2,1,0:T(8,128)(2,1)} %bitcast.7, bf16[32,3,128,128]{3,2,1,0:T(8,128)(2,1)} %tiles_in.1, ...), custom_call_target="tpu_custom_call" | custom-call | flops 4000000000 | bytes 9000000 | tf_op jit(solution)/shard_map/pallas_call | solution.py:483
  77.0 1.8 %shard_map.128 = (bf16[4096,128]{1,0:T(8,128)(2,1)}, f32[4096,128]{1,0:T(8,128)}, f32[2,256,128]{2,1,0:T(8,128)}, f32[2,128]{1,0:T(2,128)}, f32[2,128,128]{2,1,0:T(8,128)}, /*index=5*/f32[2,128]{1,0:T(2,128)}) custom-call(bf16[4096,128]{1,0:T(8,128)(2,1)S(1)} %bitcast.6, f32[4096,128]{1,0:T(8,128)S(1)} %bitcast.5, ...), custom_call_target="tpu_custom_call" | custom-call | tf_op jit(solution)/shard_map/pallas_call | solution.py:540

commit v4 on v3

--- a/solution.py
+++ b/solution.py
@@ -305,7 +305,7 @@
         lax.fori_loop(0, CH, body, 0, unroll=4)
         hold(to_right(2 + y, c, out_hi.at[y, pl.ds(c * CH, CH)]))
 
-    def inside():
+    def inside(between=None):
         def body(t, carry):
             chain(seg_c, t, tab[PREV_C + t], dot_tn(tiles[t, 2], gagg[t]))
             return carry
@@ -318,6 +318,9 @@
             return carry
 
         lax.fori_loop(0, HALO, body2, 0, unroll=16)
+
+        if between is not None:
+            between()
 
         def body3(j, carry):
             gacc[j] += (
@@ -426,6 +429,8 @@
             return carry
 
         lax.fori_loop(0, 2 * CH // RB, body2, 0, unroll=2)
+        if s == NCH - 1:
+            reduce_line_start(0)
         reach(s)
         if s < EARLY_BACK:
             pack_low(1, s)
@@ -433,15 +438,13 @@
             release()
         if s == 2:
             reduce_plane_start(1)
-    reduce_line_start(0)
     for s in range(EARLY_BACK, NCH):
         pack_low(1, s)
         pack_high(1, NCH - 1 - s)
         if s < EARLY_BACK + 2:
             ahead = (*ahead, release()) if s > EARLY_BACK else (release(),)
     gather_start(1)
-    inside()
-    reduce_plane_start(0)
+    inside(functools.partial(reduce_plane_start, 0))
     release(ahead[0])
     while held:
         ahead = (ahead[1], release(ahead[1]))

time: 79.1 us -> 77.9 us (0.985)
  Pallas kernels: 78.2 us -> 76.9 us
    pallas_call x1, Pallas kernels: 76.4 us -> 75.1 us  [per_device(): pl.pallas_call(functools.partial(main_kernel, scale), out_shape=(pltpu.VM...]
where the time goes in v4:
time: 77.9 us; the launch traced here: 77.8 us
  Pallas kernels  76.9 us (99%)
  between operations  0.8 us (1%)
    pallas_call x1, Pallas kernels, per_device(): pl.pallas_call(functools.partial(main_kernel, scale), out_shape=(pltpu.VM...  75.1 us
    pallas_call x1, Pallas kernels, per_device(): pl.pallas_call(publish_kernel, out_shape=tuple((jax.ShapeDtypeStruct(o.sh...  1.84 us

profile of v4, /device:TPU:1, one launch (start us, length us, event | category | flops | bytes accessed | tf_op | source)
XLA Modules:
  0.0 77.8 jit_solution(10115258028750900094)
XLA Ops:
  0.6 75.1 %shard_map.127 = (bf16[32,128,128]{2,1,0:T(8,128)(2,1)S(1)}, f32[32,128,128]{2,1,0:T(8,128)S(1)}, f32[2,256,128]{2,1,0:T(8,128)S(1)}, f32[2,128]{1,0:T(2,128)S(1...) custom-call(bf16[32,128,128]{2,1,0:T(8,128)(2,1)} %bitcast.7, bf16[32,3,128,128]{3,2,1,0:T(8,128)(2,1)} %tiles_in.1, ...), custom_call_target="tpu_custom_call" | custom-call | flops 4000000000 | bytes 9000000 | tf_op jit(solution)/shard_map/pallas_call | solution.py:486
  75.8 1.8 %shard_map.128 = (bf16[4096,128]{1,0:T(8,128)(2,1)}, f32[4096,128]{1,0:T(8,128)}, f32[2,256,128]{2,1,0:T(8,128)}, f32[2,128]{1,0:T(2,128)}, f32[2,128,128]{2,1,0:T(8,128)}, /*index=5*/f32[2,128]{1,0:T(2,128)}) custom-call(bf16[4096,128]{1,0:T(8,128)(2,1)S(1)} %bitcast.6, f32[4096,128]{1,0:T(8,128)S(1)} %bitcast.5, ...), custom_call_target="tpu_custom_call" | custom-call | tf_op jit(solution)/shard_map/pallas_call | solution.py:543
